TPU v7x, 32 devices: a whole 2x2x4 slice. The times are simulated.
32 devices in a mesh: groups: 2 (over y), ctx: 4 (over x, core), head: 4 (over z).
Axes of the slice: x: 2, y: 2, z: 4, core: 2. Of those that a mesh axis runs over, the one named last changes fastest.
Arguments:
- tokens_in: bfloat16 [8192, 4096], P(('groups', 'ctx')), parts along dimension 0, may hold values from -16 to 16
- tempo_ids: int32 [8192], P(('groups', 'ctx')), parts along dimension 0, may hold values from 0 to 63
- tempo_table: bfloat16 [64, 4096], replicated, may hold values from -6 to 6
- w_query: bfloat16 [4096, 2048], P('ctx', 'head'), may hold values from -0.1875 to 0.1875
- w_key: bfloat16 [4096, 2048], P('ctx', 'head'), may hold values from -0.09375 to 0.09375
- w_value: bfloat16 [4096, 2048], P('ctx', 'head'), may hold values from -0.09375 to 0.09375
Outputs:
- attended: bfloat16 [8192, 2048], P(('groups', 'ctx'), 'head'), parts along dimension 0
There are 2 independent parts, one for each index of `groups`. A program takes and returns all parts, laid end to end along the dimension named above; an argument that names none is the same for every part. Nothing has to cross between parts.
All inputs are finite; a program needn't handle non-finite values.
Results may differ from a plain program's by a relative error of at most 0.029.
Values may be sent and summed in bfloat16 or wider, within the bound.
A program may use at most 64 MiB of HBM per device.

v0:
```python
import jax
import jax.numpy as jnp
from jax import lax
from jax.sharding import PartitionSpec as P

HEAD_DIM = 128
SPAN = 1024
BEACONS = 32
POOL = 32


LOWEST = -1e30


def by_heads(matrix, heads_local):
    return matrix.reshape(matrix.shape[0], heads_local, -1).transpose(1, 0, 2)


def partial_attend(queries, keys, values, allowed):
    scores = jnp.einsum(
        "hqd,hkd->hqk", queries, keys, preferred_element_type=jnp.float32
    ) * queries.shape[-1] ** (-0.5)
    masked = jnp.where(allowed, scores, LOWEST)
    highest = jnp.max(masked, axis=2)
    weights = jnp.where(allowed, jnp.exp(masked - highest[..., None]), 0.0)
    totals = jnp.sum(weights, axis=2)
    summed = jnp.einsum(
        "hqk,hkd->hqd", weights.astype(jnp.bfloat16), values, preferred_element_type=jnp.float32
    )
    return (highest, totals, summed)


def combine_partials(first, second):
    highest = jnp.maximum(first[0], second[0])
    left_factor = jnp.exp(first[0] - highest)
    right_factor = jnp.exp(second[0] - highest)
    totals = first[1] * left_factor + second[1] * right_factor
    summed = first[2] * left_factor[..., None] + second[2] * right_factor[..., None]
    return (highest, totals, summed)


def beacon_partial(
    queries, query_span, beacon_keys, beacon_values, low_rank, high_rank, group, slots_dev
):
    heads_local, query_count, head_size = queries.shape
    block_width = group * slots_dev
    start_state = (
        jnp.full((heads_local, query_count), LOWEST, jnp.float32),
        jnp.zeros((heads_local, query_count), jnp.float32),
        jnp.zeros((heads_local, query_count, head_size), jnp.float32),
    )

    def visit(block, state):
        first_slot = block * block_width
        block_keys = lax.dynamic_slice_in_dim(beacon_keys, first_slot, block_width, 1)
        block_values = lax.dynamic_slice_in_dim(beacon_values, first_slot, block_width, 1)
        slot_index = first_slot + jnp.arange(block_width, dtype=jnp.int32)
        owner = slot_index // slots_dev
        in_range = (owner >= low_rank) & (owner < high_rank)
        earlier = (slot_index // BEACONS)[None, :] < query_span[:, None]
        allowed = (in_range[None, :] & earlier)[None]
        return combine_partials(state, partial_attend(queries, block_keys, block_values, allowed))

    first_block = low_rank // group
    last_block = (high_rank + group - 1) // group
    return lax.fori_loop(first_block, last_block, visit, start_state)


def on_device(tokens_in, tempo_ids, tempo_table, w_query, w_key, w_value):
    row_count = tokens_in.shape[0]
    col_width = w_query.shape[1]
    heads_local = col_width // HEAD_DIM
    ctx_count = lax.axis_size("ctx")
    ctx_rank = lax.axis_index("ctx")
    spans_dev = row_count // SPAN
    slots_dev = spans_dev * BEACONS
    target = max(1, 256 // slots_dev)
    group = min(ctx_count, 1 << target.bit_length() - 1)
    selector = (
        tempo_ids[:, None] == jnp.arange(tempo_table.shape[0], dtype=jnp.int32)[None, :]
    ).astype(jnp.bfloat16)
    hidden = (
        tokens_in.astype(jnp.float32)
        + jnp.dot(selector, tempo_table, preferred_element_type=jnp.float32)
    ).astype(jnp.bfloat16)
    pieces = (
        lax.all_gather(w_query, "ctx", axis=0, tiled=True),
        lax.all_gather(w_key, "ctx", axis=0, tiled=True),
        lax.all_gather(w_value, "ctx", axis=0, tiled=True),
    )
    projected = tuple(
        (jnp.dot(hidden, piece, preferred_element_type=jnp.float32) for piece in pieces)
    )
    queries = projected[0].astype(jnp.bfloat16)
    keys = projected[1].astype(jnp.bfloat16)
    values = projected[2].astype(jnp.bfloat16)
    pool_scale = POOL ** (-0.5)
    own_keys = (
        jnp.sum(keys.reshape(slots_dev, POOL, col_width).astype(jnp.float32), axis=1) * pool_scale
    ).astype(jnp.bfloat16)
    own_values = (
        jnp.sum(values.reshape(slots_dev, POOL, col_width).astype(jnp.float32), axis=1) * pool_scale
    ).astype(jnp.bfloat16)
    every_keys, every_values = (
        lax.all_gather(own_keys, "ctx", axis=0, tiled=True),
        lax.all_gather(own_values, "ctx", axis=0, tiled=True),
    )
    beacon_keys = by_heads(every_keys, heads_local)
    beacon_values = by_heads(every_values, heads_local)
    query_heads = by_heads(queries, heads_local)
    local_span = jnp.arange(row_count, dtype=jnp.int32) // SPAN
    own_span = ctx_rank * spans_dev + local_span

    def fold_spans(matrix):
        return by_heads(matrix, heads_local)

    causal = (
        jnp.arange(SPAN, dtype=jnp.int32)[:, None] >= jnp.arange(SPAN, dtype=jnp.int32)[None, :]
    )[None]
    inside = partial_attend(fold_spans(queries), fold_spans(keys), fold_spans(values), causal)
    inside = (inside[0], inside[1], inside[2])
    upper_rank = ctx_rank + 1
    remote = beacon_partial(
        query_heads,
        own_span,
        beacon_keys,
        beacon_values,
        jnp.zeros((), jnp.int32),
        upper_rank,
        group,
        slots_dev,
    )
    highest, totals, summed = combine_partials(inside, remote)
    attended = summed / totals[..., None]
    return attended.transpose(1, 0, 2).reshape(row_count, col_width).astype(jnp.bfloat16)


def solution(mesh):
    in_specs = (
        P(("groups", "ctx"), None),
        P(("groups", "ctx")),
        P(),
        P("ctx", "head"),
        P("ctx", "head"),
        P("ctx", "head"),
    )
    out_specs = P(("groups", "ctx"), "head")
    return jax.shard_map(
        on_device, mesh=mesh, in_specs=in_specs, out_specs=out_specs, check_vma=False
    )
```

profile of v0, /device:TPU:0, one launch (start us, length us, event | category | flops | bytes accessed | tf_op | source)
XLA Modules:
  0.0 165.7 jit_solution(11830383064842661481)
XLA Ops:
  6.5 0.0 copy-start
  6.5 0.0 copy-start.3
  6.5 0.0 all-gather.4.cloned.1.call-start
  6.5 0.7 all-gather.4.cloned.1.call-update
  7.3 0.0 all-gather.6.cloned.1.call-start
  7.3 0.7 all-gather.6.cloned.1.call-update
  8.0 0.0 all-gather.8.cloned.1.call-start
  8.1 0.7 all-gather.8.cloned.1.call-update
  8.8 1.3 iota_compare_fusion
  10.0 0.0 copy-done
  10.0 0.0 copy-done.3
  10.0 6.9 %add_convert_fusion = bf16[1024,4096]{1,0:T(8,128)(2,1)} fusion(bf16[1024,4096]{1,0:T(8,128)(2,1)} %param.8, bf16[64,4096]{1,0:T(8,128)(2,1)S(1)} %copy-done, s32[1024]{0:T(1024)S(1)} %copy-done.3), kind=kOutput, calls=%fused_computation.34 | convolution fusion | flops 549519360 | bytes 17305600 | tf_op jit(solution)/shard_map/dot_general | solution.py:84
  16.9 29.2 %all-gather.4.cloned.1.call-done = bf16[4096,512]{1,0:T(8,128)(2,1)} async-done(((bf16[1024,512]{1,0:T(8,128)(2,1)}), bf16[4096,512]{1,0:T(8,128)(2,1)}) %all-gather.4.cloned.1.call-update) | async-done | bytes 4194320 | tf_op jit(solution)/shard_map/all_gather | solution.py:87
  46.1 9.1 %convolution_convert_fusion.2 = bf16[1024,512]{0,1:T(8,128)(2,1)S(1)} fusion(bf16[1024,4096]{1,0:T(8,128)(2,1)} %add_convert_fusion, bf16[4096,512]{1,0:T(8,128)(2,1)} %all-gather.4.cloned.1.call-done), kind=kOutput, calls=%fused_computation.46 | convolution fusion | flops 4295491584 | bytes 13631488 | tf_op jit(solution)/shard_map/dot_general | solution.py:92
  55.2 1.3 copy.24
  56.5 25.7 %all-gather.6.cloned.1.call-done = bf16[4096,512]{1,0:T(8,128)(2,1)} async-done(((bf16[1024,512]{1,0:T(8,128)(2,1)}), bf16[4096,512]{1,0:T(8,128)(2,1)}) %all-gather.6.cloned.1.call-update) | async-done | bytes 4194320 | tf_op jit(solution)/shard_map/all_gather | solution.py:88
  82.2 10.0 %convert_reduce_fusion.1 = (f32[32,512]{1,0:T(8,128)S(1)}, bf16[1024,512]{1,0:T(8,128)(2,1)}) fusion(bf16[1024,4096]{1,0:T(8,128)(2,1)} %add_convert_fusion, bf16[4096,512]{1,0:T(8,128)(2,1)} %all-gather.6.cloned.1.call-done), kind=kOutput, calls=%fused_computation.42 | convolution fusion | flops 4296523776 | bytes 13697024 | tf_op jit(solution)/shard_map/dot_general | solution.py:92
  92.3 6.4 %all_gather.18 = bf16[128,512]{1,0:T(8,128)(2,1)S(1)} all-gather(bf16[32,512]{1,0:T(8,128)(2,1)S(1)} %multiply_convert_fusion.1), channel_id=1, replica_groups=mesh['groups'=2,'ctx'=4,'head'=4] {'ctx'}, dimensions={0}, use_global_device_ids=true | all-gather | bytes 163840 | tf_op jit(solution)/shard_map/all_gather | solution.py:105
  98.6 0.1 copy.28
  98.7 0.1 copy.30
  98.9 20.1 %all-gather.8.cloned.1.call-done = bf16[4096,512]{1,0:T(8,128)(2,1)} async-done(((bf16[1024,512]{1,0:T(8,128)(2,1)}), bf16[4096,512]{1,0:T(8,128)(2,1)}) %all-gather.8.cloned.1.call-update) | async-done | bytes 4194320 | tf_op jit(solution)/shard_map/all_gather | solution.py:89
  119.0 10.1 %convert_reduce_fusion = (f32[32,512]{1,0:T(8,128)S(1)}, bf16[1024,512]{1,0:T(8,128)(2,1)}) fusion(bf16[1024,4096]{1,0:T(8,128)(2,1)} %add_convert_fusion, bf16[4096,512]{1,0:T(8,128)(2,1)} %all-gather.8.cloned.1.call-done), kind=kOutput, calls=%fused_computation.41 | convolution fusion | flops 4296523776 | bytes 13697024 | tf_op jit(solution)/shard_map/dot_general | solution.py:92
  129.1 5.4 %all_gather.19 = bf16[128,512]{1,0:T(8,128)(2,1)S(1)} all-gather(bf16[32,512]{1,0:T(8,128)(2,1)S(1)} %multiply_convert_fusion), channel_id=1, replica_groups=mesh['groups'=2,'ctx'=4,'head'=4] {'ctx'}, dimensions={0}, use_global_device_ids=true | all-gather | bytes 163840 | tf_op jit(solution)/shard_map/all_gather | solution.py:106
  134.5 0.1 copy.29
  134.6 0.1 copy.31
  134.8 0.1 broadcast_in_dim.78
  134.9 5.2 %while.17 = (s32[]{:T(128)}, f32[4,1024]{1,0:T(4,128)S(1)}, f32[4,1024]{1,0:T(4,128)S(1)}, f32[4,1024,128]{2,1,0:T(8,128)S(1)}, s32[]{:T(128)}, /*index=5*/s32[]...) while((s32[]{:T(128)}, f32[4,1024]{1,0:T(4,128)S(1)}, ...), condition=%wide.region_6.7_spmd.clone, body=%wide.region_3.6_spmd.clone.sunk | while | flops 277116288 | bytes 12559769 | solution.py:66
  135.0 0.2 compare_and_fusion.5
  135.2 1.8 %fusion.61 = (f32[4,1024]{1,0:T(4,128)S(1)}, f32[4,1024,128]{1,2,0:T(8,128)S(1)}) fusion(pred[1024,128]{0,1:T(8,128)(4,1)S(1)} %compare_and_fusion.5, bf16[4,1024,128]{2,1,0:T(8,128)(2,1)} %get-tuple-element.322, bf16[4,128,128]{2,1,0:T(8,128)(2,1)S(1)} %get-tuple-element.323), kind=kOutput, calls=%fused_computation.4.clone.1 | convolution fusion | flops 135786496 | bytes 3424256 | tf_op jit(solution)/shard_map/while/body/hqd,hkd->hqk/dot_general | solution.py:20
  137.0 0.6 fusion.62
  137.6 2.5 %multiply_add_fusion.6 = f32[4,1024,128]{2,1,0:T(8,128)S(1)} fusion(f32[4,1024,128]{2,1,0:T(8,128)S(1)} %get-tuple-element.307, bf16[4,128,128]{2,1,0:T(8,128)(2,1)S(1)} %get-tuple-element.324, f32[4,1024,128]{1,2,0:T(8,128)S(1)} %get-tuple-element.286, f32[4,1024]{1,0:T(4,128)S(1)} %get-tuple-element.290, f32[4,1024]{1,0:T(4,128)S(1)} %get-tuple-element.291, ...), kind=kOutput, calls=%fused_computation.1.clone.1 | convolution fusion | flops 138412032 | bytes 6602752 | tf_op jit(solution)/shard_map/while/body/hqk,hkd->hqd/dot_general | solution.py:27
  140.1 1.9 %copy.32 = f32[4,1024,128]{1,2,0:T(8,128)} copy(f32[4,1024,128]{2,1,0:T(8,128)S(1)} %get-tuple-element.137) | data formatting | bytes 4194304 | tf_op jit(solution)/shard_map/while | solution.py:66
  142.0 1.5 copy.36
  143.5 0.0 copy-start.1
  143.5 5.0 %fusion.18 = (f32[4,1024]{1,0:T(4,128)S(1)}, f32[4,1024,1024]{1,2,0:T(8,128)S(1)}) fusion(pred[1024,1024]{0,1:T(8,128)(4,1)} %iota_compare_fusion, bf16[1024,4,128]{2,0,1:T(8,128)(2,1)} %bitcast.56, bf16[1024,512]{1,0:T(8,128)(2,1)} %get-tuple-element.213), kind=kOutput, calls=%fused_computation.35 | convolution fusion | flops 1086320640 | bytes 19939328 | tf_op jit(solution)/shard_map/hqd,hkd->hqk/dot_general | solution.py:20
  148.5 0.0 copy-done.1
  148.5 0.0 copy-start.2
  148.5 4.2 %fusion.19 = f32[4,1024]{1,0:T(4,128)S(1)} fusion(f32[4,1024,1024]{1,2,0:T(8,128)S(1)} %get-tuple-element.217, f32[4,1024]{1,0:T(4,128)S(1)} %get-tuple-element.216, pred[1024,1024]{0,1:T(8,128)(4,1)S(1)} %copy-done.1), kind=kLoop, calls=%fused_computation.36 | loop fusion | flops 20967424 | bytes 17858560 | tf_op jit(solution)/shard_map/reduce_sum | solution.py:26
  152.7 0.0 copy-done.2
  152.7 5.1 %divide_convert_fusion = bf16[4,1024,128]{1,2,0:T(8,128)(2,1)S(1)} fusion(f32[4,1024,128]{1,2,0:T(8,128)S(1)} %copy-done.2, bf16[4,1024,128]{1,2,0:T(8,128)(2,1)S(1)} %bitcast.57, f32[4,1024,1024]{1,2,0:T(8,128)S(1)} %get-tuple-element.217, f32[4,1024]{1,0:T(4,128)S(1)} %get-tuple-element.216, pred[1024,1024]{0,1:T(8,128)(4,1)S(1)} %copy-done.1, ...), kind=kOutput, calls=%fused_computation.43 | convolution fusion | flops 1097334784 | bytes 22085632 | tf_op jit(solution)/shard_map/hqk,hkd->hqd/dot_general | solution.py:27
  157.8 1.3 copy.33
  (9 shorter events, 0.1 us)
Async XLA Ops:
  6.5 3.5 %copy-start = (bf16[64,4096]{1,0:T(8,128)(2,1)S(1)}, bf16[64,4096]{1,0:T(8,128)(2,1)}, u32[]{:S(2)}) copy-start(bf16[64,4096]{1,0:T(8,128)(2,1)} %param.10) | copy-start | bytes 1572868
  6.5 3.5 %copy-start.3 = (s32[1024]{0:T(1024)S(1)}, s32[1024]{0:T(1024)}, u32[]{:S(2)}) copy-start(s32[1024]{0:T(1024)} %param.9) | copy-start | bytes 12292
  6.5 39.6 %all-gather.4.cloned.1.call-start = ((), (), s32[]{:S(2)}) async-start(), calls=%async_computation | async-start | bytes 5242880 | tf_op jit(solution)/shard_map/all_gather | solution.py:87
  7.3 74.9 %all-gather.6.cloned.1.call-start = ((), (), s32[]{:S(2)}) async-start(), calls=%async_computation.1 | async-start | bytes 5242880 | tf_op jit(solution)/shard_map/all_gather | solution.py:88
  8.0 111.0 %all-gather.8.cloned.1.call-start = ((), (), s32[]{:S(2)}) async-start(), calls=%async_computation.2 | async-start | bytes 5242880 | tf_op jit(solution)/shard_map/all_gather | solution.py:89
  143.5 5.0 %copy-start.1 = (pred[1024,1024]{0,1:T(8,128)(4,1)S(1)}, pred[1024,1024]{0,1:T(8,128)(4,1)}, u32[]{:S(2)}) copy-start(pred[1024,1024]{0,1:T(8,128)(4,1)} %iota_compare_fusion) | copy-start | bytes 3145732
  148.5 4.2 %copy-start.2 = (f32[4,1024,128]{1,2,0:T(8,128)S(1)}, f32[4,1024,128]{1,2,0:T(8,128)}, u32[]{:S(2)}) copy-start(f32[4,1024,128]{1,2,0:T(8,128)} %copy.32) | copy-start | bytes 6291460
Sparse Core Ops, SparseCore 0:
  8.9 37.1 all-gather.3
  47.7 34.4 all-gather.5
  83.8 35.1 all-gather.7
where the time goes:
time: 166 us
  waiting for transfers between devices  77.1 us (46%)
  matrix products  50.5 us (30%)
  between operations  13.3 us (8%)
  blocking collectives  11.8 us (7%)
  local copies, waits for them, and re-layouts  6.65 us (4%)
  other arithmetic  6.29 us (4%)
    dot_general x3, matrix products, on_device(): jnp.dot(hidden, piece, preferred_element_type=jnp.float32)  29.2 us
    all_gather x1, waiting for transfers between devices, on_device(): lax.all_gather(w_query, 'ctx', axis=0, tiled=True)  29.2 us
    all_gather x1, waiting for transfers between devices, on_device(): lax.all_gather(w_key, 'ctx', axis=0, tiled=True)  25.7 us
    all_gather x1, waiting for transfers between devices, on_device(): lax.all_gather(w_value, 'ctx', axis=0, tiled=True)  20.1 us
    dot_general x2, matrix products, partial_attend(): jnp.einsum('hqk,hkd->hqd', weights.astype(jnp.bfloat16), values, preferre...  7.61 us
    dot_general x1, matrix products, on_device(): jnp.dot(selector, tempo_table, preferred_element_type=jnp.float32)  6.89 us
    dot_general x2, matrix products, partial_attend(): jnp.einsum('hqd,hkd->hqk', queries, keys, preferred_element_type=jnp.floa...  6.76 us
    all_gather x1, blocking collectives, on_device(): lax.all_gather(own_keys, 'ctx', axis=0, tiled=True)  6.35 us
  transfers between devices with their start and end apart: 3, of which 3 were waited for; matrix products, arithmetic and copies ran while one was open for 17% of the time, Pallas kernels for 0%

commit v1 on v0

--- a/solution.py
+++ b/solution.py
@@ -1,6 +1,11 @@
+import functools
+import math
+
 import jax
 import jax.numpy as jnp
 from jax import lax
+from jax.experimental import pallas as pl
+from jax.experimental.pallas import tpu as pltpu
 from jax.sharding import PartitionSpec as P
 
 HEAD_DIM = 128
@@ -135,7 +140,437 @@
     return attended.transpose(1, 0, 2).reshape(row_count, col_width).astype(jnp.bfloat16)
 
 
+CHUNK = HEAD_DIM
+PAIR = 2 * HEAD_DIM
+AHEAD = 3
+MESH = pl.DeviceIdType.MESH
+QUERY, KEY, VALUE = 0, 1, 2
+
+
+def song_kernel(
+    tokens_hbm,
+    ids_ref,
+    table_ref,
+    wq_hbm,
+    wk_hbm,
+    wv_hbm,
+    out_ref,
+    hidden,
+    weights,
+    partial,
+    rounded,
+    selector,
+    beacons,
+    token_sem,
+    own_sem,
+    x_send,
+    x_recv,
+    y_send,
+    y_recv,
+    own_send,
+    own_recv,
+    cx_send,
+    cx_recv,
+    cy_send,
+    cy_recv,
+    b_send,
+    b_recv,
+):
+    rows, depth = hidden.shape
+    shard, width = wq_hbm.shape
+    pairs = width // PAIR
+    half = shard // 2
+    near = 2 * shard
+    sources = (wq_hbm, wk_hbm, wv_hbm)
+
+    song = lax.axis_index("groups")
+    rank = lax.axis_index("ctx")
+    chip, core = rank // 2, rank % 2
+    far_chip = 1 - chip
+    sibling = {"ctx": chip * 2 + 1 - core}
+    across = {"ctx": far_chip * 2 + core}
+    diagonal = {"ctx": far_chip * 2 + 1 - core}
+    twin = {"groups": 1 - song}
+
+    near_row = pl.multiple_of(chip * near, near)
+    far_row = pl.multiple_of(far_chip * near, near)
+    units = [(kind, pair) for pair in range(pairs) for kind in (KEY, VALUE, QUERY)]
+    chunks = [(kind, pair * 2 + side) for kind, pair in units for side in range(2)]
+    count = len(chunks)
+
+    def spot(index, owner_chip, owner_core, part):
+        kind, block = chunks[index]
+        row = pl.multiple_of((owner_chip * 2 + owner_core) * shard + part * half, half)
+        return weights.at[kind, pl.ds(row, half), pl.ds(block * CHUNK, CHUNK)]
+
+    def x_copy(index):
+        kind, block = chunks[index]
+        begin = pl.multiple_of(song * half, half)
+        return pltpu.make_async_remote_copy(
+            src_ref=sources[kind].at[pl.ds(begin, half), pl.ds(block * CHUNK, CHUNK)],
+            dst_ref=spot(index, chip, core, song),
+            send_sem=x_send.at[index],
+            recv_sem=x_recv.at[index],
+            device_id=across,
+            device_id_type=MESH,
+        )
+
+    def y_copy(index):
+        place = spot(index, far_chip, core, song)
+        return pltpu.make_async_remote_copy(
+            src_ref=place,
+            dst_ref=place,
+            send_sem=y_send.at[index],
+            recv_sem=y_recv.at[index],
+            device_id=twin,
+            device_id_type=MESH,
+        )
+
+    def core_copy(index, part, send, recv):
+        place = spot(index, far_chip, core, part)
+        return pltpu.make_async_remote_copy(
+            src_ref=place,
+            dst_ref=place,
+            send_sem=send.at[index],
+            recv_sem=recv.at[index],
+            device_id=sibling,
+            device_id_type=MESH,
+        )
+
+    def cx_copy(index):
+        return core_copy(index, song, cx_send, cx_recv)
+
+    def cy_copy(index):
+        return core_copy(index, 1 - song, cy_send, cy_recv)
+
+    def own_place(unit):
+        kind, pair = units[unit]
+        row = pl.multiple_of(rank * shard, shard)
+        return weights.at[kind, pl.ds(row, shard), pl.ds(pair * PAIR, PAIR)]
+
+    def own_source(unit):
+        kind, pair = units[unit]
+        return sources[kind].at[:, pl.ds(pair * PAIR, PAIR)]
+
+    def own_copy(unit):
+        return pltpu.make_async_copy(own_source(unit), own_place(unit), own_sem.at[unit])
+
+    def own_remote(unit):
+        return pltpu.make_async_remote_copy(
+            src_ref=own_source(unit),
+            dst_ref=own_place(unit),
+            send_sem=own_send.at[unit],
+            recv_sem=own_recv.at[unit],
+            device_id=sibling,
+            device_id_type=MESH,
+        )
+
+    token_step = depth // 4
+
+    def token_copy(block):
+        row = near_row if block < 2 else far_row
+        start = pl.multiple_of(row + (block % 2) * token_step, token_step)
+        place = pl.ds(start, token_step)
+        return pltpu.make_async_copy(
+            tokens_hbm.at[:, place], hidden.at[:, place], token_sem.at[block]
+        )
+
+    def beacon_copies(kind, pair):
+        place = beacons.at[kind - 1, pair, pl.ds(pl.multiple_of(rank * BEACONS, BEACONS), BEACONS)]
+        result = []
+        for number, target in enumerate((sibling, across, diagonal)):
+            result.append(
+                pltpu.make_async_remote_copy(
+                    src_ref=place,
+                    dst_ref=place,
+                    send_sem=b_send.at[kind - 1, pair, number],
+                    recv_sem=b_recv.at[kind - 1, pair, number],
+                    device_id=target,
+                    device_id_type=MESH,
+                )
+            )
+        return result
+
+    token_copy(0).start()
+    token_copy(1).start()
+    barrier = pltpu.get_barrier_semaphore()
+    partners = (sibling, across, diagonal, twin)
+    for target in partners:
+        pl.semaphore_signal(barrier, inc=1, device_id=target, device_id_type=MESH)
+    pl.semaphore_wait(barrier, len(partners))
+
+    for index in range(AHEAD):
+        x_copy(index).start()
+    for unit in range(len(units)):
+        own_remote(unit).start()
+    token_copy(2).start()
+    token_copy(3).start()
+    for unit in range(len(units)):
+        own_copy(unit).start()
+
+    tempos = table_ref.shape[0]
+    picked = lax.broadcasted_iota(jnp.int32, (tempos, rows), 0) == ids_ref[...]
+    selector[...] = picked.astype(jnp.float32).T.astype(jnp.bfloat16)
+
+    def make_hidden(block):
+        token_copy(block).wait()
+        row = near_row if block < 2 else far_row
+        start = pl.multiple_of(row + (block % 2) * token_step, token_step)
+        place = pl.ds(start, token_step)
+
+        @pl.loop(0, rows // 256)
+        def _(tile):
+            lines = pl.ds(pl.multiple_of(tile * 256, 256), 256)
+            added = jnp.dot(
+                selector[lines, :], table_ref[:, place], preferred_element_type=jnp.float32
+            )
+            hidden[lines, place] = (hidden[lines, place].astype(jnp.float32) + added).astype(
+                jnp.bfloat16
+            )
+
+    tall = rows // 2
+
+    def near_product(unit):
+        own_copy(unit).wait()
+        own_remote(unit).wait_recv()
+        kind, pair = units[unit]
+        cols = pl.ds(pair * PAIR, PAIR)
+
+        @pl.loop(0, 2)
+        def _(tile):
+            lines = pl.ds(pl.multiple_of(tile * tall, tall), tall)
+            partial[kind, lines, cols] = jnp.dot(
+                hidden[lines, pl.ds(near_row, near)],
+                weights[kind, pl.ds(near_row, near), cols],
+                preferred_element_type=jnp.float32,
+            )
+
+    def far_product(kind, first, size):
+        cols = pl.ds(first, size)
+
+        @pl.loop(0, 2)
+        def _(tile):
+            lines = pl.ds(pl.multiple_of(tile * tall, tall), tall)
+            rounded[kind, lines, cols] = (
+                partial[kind, lines, cols]
+                + jnp.dot(
+                    hidden[lines, pl.ds(far_row, near)],
+                    weights[kind, pl.ds(far_row, near), cols],
+                    preferred_element_type=jnp.float32,
+                )
+            ).astype(jnp.bfloat16)
+
+    def share_beacons(kind, pair):
+        slots = lax.broadcasted_iota(jnp.int32, (BEACONS, rows), 0)
+        owner = lax.broadcasted_iota(jnp.int32, (BEACONS, rows), 1) // POOL
+        pooling = (slots == owner).astype(jnp.bfloat16)
+        pooled = jnp.dot(
+            pooling,
+            rounded[kind, :, pl.ds(pair * PAIR, PAIR)],
+            preferred_element_type=jnp.float32,
+        ) * POOL ** (-0.5)
+        place = pl.ds(pl.multiple_of(rank * BEACONS, BEACONS), BEACONS)
+        beacons[kind - 1, pair, place, :] = pooled.astype(jnp.bfloat16)
+        for copy in beacon_copies(kind, pair):
+            copy.start()
+
+    def await_beacons(pair):
+        for kind in (KEY, VALUE):
+            for copy in beacon_copies(kind, pair):
+                copy.wait_recv()
+
+    slot_count = beacons.shape[2]
+    factor = HEAD_DIM ** (-0.5) * math.log2(math.e)
+    block_rows = 256
+    contract_last = (((1,), (1,)), ((), ()))
+
+    def attend(head):
+        pair, side = head // 2, head % 2
+        cols = pl.ds(head * HEAD_DIM, HEAD_DIM)
+        inner = pl.ds(side * HEAD_DIM, HEAD_DIM)
+        far_keys = beacons[0, pair, :, inner]
+        far_values = beacons[1, pair, :, inner]
+        earlier = lax.broadcasted_iota(jnp.int32, (block_rows, slot_count), 1) < rank * BEACONS
+        causal = lax.broadcasted_iota(
+            jnp.int32, (block_rows, block_rows), 0
+        ) >= lax.broadcasted_iota(jnp.int32, (block_rows, block_rows), 1)
+        for block in range(rows // block_rows):
+            lines = pl.ds(block * block_rows, block_rows)
+            query = rounded[QUERY, lines, cols]
+            parts = [
+                (
+                    jnp.where(
+                        earlier,
+                        lax.dot_general(
+                            query, far_keys, contract_last, preferred_element_type=jnp.float32
+                        ),
+                        LOWEST,
+                    ),
+                    far_values,
+                ),
+                (
+                    jnp.where(
+                        causal,
+                        lax.dot_general(
+                            query,
+                            rounded[KEY, lines, cols],
+                            contract_last,
+                            preferred_element_type=jnp.float32,
+                        ),
+                        LOWEST,
+                    ),
+                    rounded[VALUE, lines, cols],
+                ),
+            ]
+            if block:
+                before = pl.ds(0, block * block_rows)
+                parts.append(
+                    (
+                        lax.dot_general(
+                            query,
+                            rounded[KEY, before, cols],
+                            contract_last,
+                            preferred_element_type=jnp.float32,
+                        ),
+                        rounded[VALUE, before, cols],
+                    )
+                )
+            highest = functools.reduce(
+                jnp.maximum, [jnp.max(score, axis=1, keepdims=True) for score, _ in parts]
+            )
+            total = 0.0
+            summed = 0.0
+            for score, value in parts:
+                weight = jnp.exp2((score - highest) * factor)
+                total = total + jnp.sum(weight, axis=1, keepdims=True)
+                summed = summed + jnp.dot(
+                    weight.astype(jnp.bfloat16), value, preferred_element_type=jnp.float32
+                )
+            out_ref[lines, cols] = (summed / total).astype(jnp.bfloat16)
+
+    def far_unit(unit):
+        kind, pair = units[unit]
+        far_product(kind, pair * PAIR, PAIR)
+        if kind != QUERY:
+            share_beacons(kind, pair)
+
+    def far_chunk(index):
+        kind, block = chunks[index]
+        far_product(kind, block * CHUNK, CHUNK)
+
+    work = {step: [] for step in range(count + 2)}
+    work[0] += [functools.partial(make_hidden, 2), functools.partial(make_hidden, 3)]
+    near_at = [1, 1, 2, 2, 4, 4]
+    for unit in range(len(units)):
+        work[near_at[min(unit, 5)]].append(functools.partial(near_product, unit))
+    for unit in range(len(units) - 1):
+        work[2 * unit + 3].append(functools.partial(far_unit, unit))
+    for pair in range(pairs - 1):
+        ready = 6 * pair + 8
+        work[ready - 1].append(functools.partial(await_beacons, pair))
+        work[ready].append(functools.partial(attend, 2 * pair))
+        work[ready + 2].append(functools.partial(attend, 2 * pair + 1))
+    work[count].append(functools.partial(far_chunk, count - 2))
+    work[count].append(functools.partial(await_beacons, pairs - 1))
+    work[count].append(functools.partial(attend, 2 * pairs - 2))
+    work[count + 1].append(functools.partial(far_chunk, count - 1))
+    work[count + 1].append(functools.partial(attend, 2 * pairs - 1))
+
+    make_hidden(0)
+    make_hidden(1)
+    for step in range(count + 2):
+        if step < count:
+            x_copy(step).wait_recv()
+            y_copy(step).start()
+            cx_copy(step).start()
+            if step + AHEAD < count:
+                x_copy(step).wait_send()
+                x_copy(step + AHEAD).start()
+        if 1 <= step <= count:
+            y_copy(step - 1).wait_recv()
+            cy_copy(step - 1).start()
+            cx_copy(step - 1).wait_recv()
+        if step >= 2:
+            cy_copy(step - 2).wait_recv()
+        for task in work[step]:
+            task()
+
+    for index in range(count):
+        if index + AHEAD >= count:
+            x_copy(index).wait_send()
+        y_copy(index).wait_send()
+        cx_copy(index).wait_send()
+        cy_copy(index).wait_send()
+    for unit in range(len(units)):
+        own_remote(unit).wait_send()
+    for pair in range(pairs):
+        for kind in (KEY, VALUE):
+            for copy in beacon_copies(kind, pair):
+                copy.wait_send()
+
+
+def on_device_fused(tokens_in, tempo_ids, tempo_table, w_query, w_key, w_value):
+    rows, depth = tokens_in.shape
+    width = w_query.shape[1]
+    pairs = width // PAIR
+    units = 3 * pairs
+    chunks = 2 * units
+    slots = lax.axis_size("ctx") * BEACONS
+    dma = pltpu.SemaphoreType.DMA
+    anywhere = pl.BlockSpec(memory_space=pl.ANY)
+    vmem = pl.BlockSpec(memory_space=pltpu.VMEM)
+    return pl.pallas_call(
+        song_kernel,
+        out_shape=jax.ShapeDtypeStruct((rows, width), jnp.bfloat16),
+        in_specs=[anywhere, vmem, vmem, anywhere, anywhere, anywhere],
+        out_specs=vmem,
+        scratch_shapes=[
+            pltpu.VMEM((rows, depth), jnp.bfloat16),
+            pltpu.VMEM((3, depth, width), jnp.bfloat16),
+            pltpu.VMEM((3, rows, width), jnp.float32),
+            pltpu.VMEM((3, rows, width), jnp.bfloat16),
+            pltpu.VMEM((rows, tempo_table.shape[0]), jnp.bfloat16),
+            pltpu.VMEM((2, pairs, slots, PAIR), jnp.bfloat16),
+            dma((4,)),
+            dma((units,)),
+            dma((chunks,)),
+            dma((chunks,)),
+            dma((chunks,)),
+            dma((chunks,)),
+            dma((units,)),
+            dma((units,)),
+            dma((chunks,)),
+            dma((chunks,)),
+            dma((chunks,)),
+            dma((chunks,)),
+            dma((2, pairs, 3)),
+            dma((2, pairs, 3)),
+        ],
+        compiler_params=pltpu.CompilerParams(
+            collective_id=0, has_side_effects=True, vmem_limit_bytes=56 * 2**20
+        ),
+        cost_estimate=pl.CostEstimate(
+            flops=2 * rows * depth * width * 3,
+            bytes_accessed=2 * (rows * depth + 3 * depth * width),
+            transcendentals=rows * rows * (width // HEAD_DIM),
+        ),
+    )(tokens_in, tempo_ids.reshape(1, rows), tempo_table, w_query, w_key, w_value)
+
+
 def solution(mesh):
+    sizes = dict(mesh.shape)
+
+    def choose(tokens_in, tempo_ids, tempo_table, w_query, w_key, w_value):
+        fused = (
+            sizes["groups"] == 2
+            and sizes["ctx"] == 4
+            and tokens_in.shape[0] == SPAN
+            and w_query.shape[0] * 4 == tokens_in.shape[1]
+            and w_query.shape[1] % PAIR == 0
+        )
+        body = on_device_fused if fused else on_device
+        return body(tokens_in, tempo_ids, tempo_table, w_query, w_key, w_value)
+
     in_specs = (
         P(("groups", "ctx"), None),
         P(("groups", "ctx")),
@@ -146,5 +581,5 @@
     )
     out_specs = P(("groups", "ctx"), "head")
     return jax.shard_map(
-        on_device, mesh=mesh, in_specs=in_specs, out_specs=out_specs, check_vma=False
-    )
+        choose, mesh=mesh, in_specs=in_specs, out_specs=out_specs, check_vma=False
+    )

time: 166 us -> 62.6 us (0.38)
  waiting for transfers between devices: 77.1 us -> 0 us
  Pallas kernels: 0 us -> 60.1 us
  matrix products: 50.5 us -> 0 us
  between operations: 13.3 us -> 0.01 us
  blocking collectives: 11.8 us -> 0 us
  other arithmetic: 6.29 us -> 0 us
  local copies, waits for them, and re-layouts: 6.65 us -> 2.26 us
    all_gather x3 -> x0, waiting for transfers between devices: 75 us -> none  [the longest x1 29.2 us: on_device(): lax.all_gather(w_query, 'ctx', axis=0, tiled=True)]
    pallas_call x0 -> x1, Pallas kernels: none -> 60.1 us  [on_device_fused(): pl.pallas_call(song_kernel, out_shape=jax.ShapeDtypeStruct((rows, width),...]
    dot_general x8 -> x0, matrix products: 50.5 us -> none  [the longest x3 29.2 us: on_device(): jnp.dot(hidden, piece, preferred_element_type=jnp.float32)]
    all_gather x2 -> x0, blocking collectives: 11.8 us -> none  [the longest x1 6.35 us: on_device(): lax.all_gather(own_keys, 'ctx', axis=0, tiled=True)]
    reduce_sum x2 -> x0, other arithmetic: 4.74 us -> none  [partial_attend(): totals = jnp.sum(weights, axis=2)]
    reshape x2 -> x0, local copies, waits for them, and re-layouts: 2.79 us -> none  [by_heads(): return matrix.reshape(matrix.shape[0], heads_local, -1).transpose(1, 0, 2)]
    unnamed x3 -> x0, waiting for transfers between devices: 2.09 us -> none
    unnamed x10 -> x1, local copies, waits for them, and re-layouts: 0.29 us -> 2.26 us
  transfers between devices with their start and end apart: 3 -> 0, of which waited for: 3 -> 0; matrix products, arithmetic and copies ran while one was open for 17% -> 0% of each run, Pallas kernels for 0% -> 0%
where the time goes in v1:
time: 62.6 us; the launch traced here: 62.4 us
  Pallas kernels  60.1 us (96%)
  local copies, waits for them, and re-layouts  2.26 us (4%)
    pallas_call x1, Pallas kernels, on_device_fused(): pl.pallas_call(song_kernel, out_shape=jax.ShapeDtypeStruct((rows, width),...  60.1 us
    unnamed x1, local copies, waits for them, and re-layouts  2.26 us

profile of v1, /device:TPU:0, one launch (start us, length us, event | category | flops | bytes accessed | tf_op | source)
XLA Modules:
  0.0 62.4 jit_solution(11983246355582318657)
XLA Ops:
  0.0 60.1 %shard_map.64 = bf16[1024,512]{1,0:T(8,128)(2,1)} custom-call(bf16[1024,4096]{1,0:T(8,128)(2,1)} %tokens_hbm.1, s32[1,1024]{1,0:T(1,128)} %bitcast.1, bf16[64,4096]{1,0:T(8,128)(2,1)} %table_ref.1, bf16[1024,512]{1,0:T(8,128)(2,1)} %wq_hbm.1, bf16[1024,512]{1,0:T(8,128)(2,1)} %wk_hbm.1, bf16[1024,512]{1,0:T(8,128)(2,1)} %wv_hbm.1), custom_call_target="tpu_custom_call" | custom-call | flops 12884901888 | bytes 20971520 | tf_op jit(solution)/shard_map/pallas_call | solution.py:522
  60.1 2.3 %copy.8 = bf16[1024,512]{1,0:T(8,128)(2,1)} copy(bf16[1024,512]{1,0:T(8,128)(2,1)} %shard_map.64) | data formatting | bytes 2097152

commit v2 on v1

--- a/solution.py
+++ b/solution.py
@@ -149,8 +149,8 @@
 
 def song_kernel(
     tokens_hbm,
-    ids_ref,
-    table_ref,
+    ids_hbm,
+    table_hbm,
     wq_hbm,
     wk_hbm,
     wv_hbm,
@@ -161,6 +161,9 @@
     rounded,
     selector,
     beacons,
+    ids_ref,
+    table_ref,
+    small_sem,
     token_sem,
     own_sem,
     x_send,
@@ -194,26 +197,42 @@
 
     near_row = pl.multiple_of(chip * near, near)
     far_row = pl.multiple_of(far_chip * near, near)
-    units = [(kind, pair) for pair in range(pairs) for kind in (KEY, VALUE, QUERY)]
-    chunks = [(kind, pair * 2 + side) for kind, pair in units for side in range(2)]
-    count = len(chunks)
+    units = 3 * pairs
+    count = 2 * units
+
+    def unit_of(unit):
+        return (unit + 1) % 3, unit // 3
+
+    def chunk_of(index):
+        kind, pair = unit_of(index // 2)
+        return kind, pair * 2 + index % 2
+
+    def columns(block, size):
+        return pl.ds(pl.multiple_of(block * size, size), size)
 
     def spot(index, owner_chip, owner_core, part):
-        kind, block = chunks[index]
+        kind, block = chunk_of(index)
         row = pl.multiple_of((owner_chip * 2 + owner_core) * shard + part * half, half)
-        return weights.at[kind, pl.ds(row, half), pl.ds(block * CHUNK, CHUNK)]
-
-    def x_copy(index):
-        kind, block = chunks[index]
+        return weights.at[kind, pl.ds(row, half), columns(block, CHUNK)]
+
+    def x_copy(index, source):
+        block = chunk_of(index)[1]
         begin = pl.multiple_of(song * half, half)
         return pltpu.make_async_remote_copy(
-            src_ref=sources[kind].at[pl.ds(begin, half), pl.ds(block * CHUNK, CHUNK)],
+            src_ref=source.at[pl.ds(begin, half), columns(block, CHUNK)],
             dst_ref=spot(index, chip, core, song),
             send_sem=x_send.at[index],
             recv_sem=x_recv.at[index],
             device_id=across,
             device_id_type=MESH,
         )
+
+    def x_start(index):
+        for kind, source in enumerate(sources):
+
+            @pl.when(chunk_of(index)[0] == kind)
+            def _():
+                x_copy(index, source).start()
 
     def y_copy(index):
         place = spot(index, far_chip, core, song)
@@ -244,13 +263,15 @@
         return core_copy(index, 1 - song, cy_send, cy_recv)
 
     def own_place(unit):
-        kind, pair = units[unit]
+        kind, pair = unit_of(unit)
         row = pl.multiple_of(rank * shard, shard)
-        return weights.at[kind, pl.ds(row, shard), pl.ds(pair * PAIR, PAIR)]
+        return weights.at[kind, pl.ds(row, shard), columns(pair, PAIR)]
 
     def own_source(unit):
-        kind, pair = units[unit]
-        return sources[kind].at[:, pl.ds(pair * PAIR, PAIR)]
+        if not isinstance(unit, int):
+            return own_place(unit)
+        kind, pair = unit_of(unit)
+        return sources[kind].at[:, columns(pair, PAIR)]
 
     def own_copy(unit):
         return pltpu.make_async_copy(own_source(unit), own_place(unit), own_sem.at[unit])
@@ -267,10 +288,13 @@
 
     token_step = depth // 4
 
+    def token_place(block):
+        side = (chip + block // 2) % 2
+        start = pl.multiple_of(side * near + (block % 2) * token_step, token_step)
+        return pl.ds(start, token_step)
+
     def token_copy(block):
-        row = near_row if block < 2 else far_row
-        start = pl.multiple_of(row + (block % 2) * token_step, token_step)
-        place = pl.ds(start, token_step)
+        place = token_place(block)
         return pltpu.make_async_copy(
             tokens_hbm.at[:, place], hidden.at[:, place], token_sem.at[block]
         )
@@ -291,6 +315,10 @@
             )
         return result
 
+    ids_copy = pltpu.make_async_copy(ids_hbm, ids_ref, small_sem.at[0])
+    table_copy = pltpu.make_async_copy(table_hbm, table_ref, small_sem.at[1])
+    ids_copy.start()
+    table_copy.start()
     token_copy(0).start()
     token_copy(1).start()
     barrier = pltpu.get_barrier_semaphore()
@@ -300,23 +328,23 @@
     pl.semaphore_wait(barrier, len(partners))
 
     for index in range(AHEAD):
-        x_copy(index).start()
-    for unit in range(len(units)):
+        x_copy(index, sources[chunk_of(index)[0]]).start()
+    for unit in range(units):
         own_remote(unit).start()
     token_copy(2).start()
     token_copy(3).start()
-    for unit in range(len(units)):
+    for unit in range(units):
         own_copy(unit).start()
 
     tempos = table_ref.shape[0]
+    ids_copy.wait()
+    table_copy.wait()
     picked = lax.broadcasted_iota(jnp.int32, (tempos, rows), 0) == ids_ref[...]
     selector[...] = picked.astype(jnp.float32).T.astype(jnp.bfloat16)
 
     def make_hidden(block):
         token_copy(block).wait()
-        row = near_row if block < 2 else far_row
-        start = pl.multiple_of(row + (block % 2) * token_step, token_step)
-        place = pl.ds(start, token_step)
+        place = token_place(block)
 
         @pl.loop(0, rows // 256)
         def _(tile):
@@ -333,32 +361,28 @@
     def near_product(unit):
         own_copy(unit).wait()
         own_remote(unit).wait_recv()
-        kind, pair = units[unit]
-        cols = pl.ds(pair * PAIR, PAIR)
+        kind, pair = unit_of(unit)
+        cols = columns(pair, PAIR)
 
         @pl.loop(0, 2)
         def _(tile):
-            lines = pl.ds(pl.multiple_of(tile * tall, tall), tall)
+            lines = columns(tile, tall)
             partial[kind, lines, cols] = jnp.dot(
                 hidden[lines, pl.ds(near_row, near)],
                 weights[kind, pl.ds(near_row, near), cols],
                 preferred_element_type=jnp.float32,
             )
 
-    def far_product(kind, first, size):
-        cols = pl.ds(first, size)
-
-        @pl.loop(0, 2)
-        def _(tile):
-            lines = pl.ds(pl.multiple_of(tile * tall, tall), tall)
-            rounded[kind, lines, cols] = (
-                partial[kind, lines, cols]
-                + jnp.dot(
-                    hidden[lines, pl.ds(far_row, near)],
-                    weights[kind, pl.ds(far_row, near), cols],
-                    preferred_element_type=jnp.float32,
-                )
-            ).astype(jnp.bfloat16)
+    def far_product(kind, cols, tile):
+        lines = columns(tile, tall)
+        rounded[kind, lines, cols] = (
+            partial[kind, lines, cols]
+            + jnp.dot(
+                hidden[lines, pl.ds(far_row, near)],
+                weights[kind, pl.ds(far_row, near), cols],
+                preferred_element_type=jnp.float32,
+            )
+        ).astype(jnp.bfloat16)
 
     def share_beacons(kind, pair):
         slots = lax.broadcasted_iota(jnp.int32, (BEACONS, rows), 0)
@@ -366,7 +390,7 @@
         pooling = (slots == owner).astype(jnp.bfloat16)
         pooled = jnp.dot(
             pooling,
-            rounded[kind, :, pl.ds(pair * PAIR, PAIR)],
+            rounded[kind, :, columns(pair, PAIR)],
             preferred_element_type=jnp.float32,
         ) * POOL ** (-0.5)
         place = pl.ds(pl.multiple_of(rank * BEACONS, BEACONS), BEACONS)
@@ -386,8 +410,8 @@
 
     def attend(head):
         pair, side = head // 2, head % 2
-        cols = pl.ds(head * HEAD_DIM, HEAD_DIM)
-        inner = pl.ds(side * HEAD_DIM, HEAD_DIM)
+        cols = columns(head, HEAD_DIM)
+        inner = columns(side, HEAD_DIM)
         far_keys = beacons[0, pair, :, inner]
         far_values = beacons[1, pair, :, inner]
         earlier = lax.broadcasted_iota(jnp.int32, (block_rows, slot_count), 1) < rank * BEACONS
@@ -448,60 +472,93 @@
                 )
             out_ref[lines, cols] = (summed / total).astype(jnp.bfloat16)
 
-    def far_unit(unit):
-        kind, pair = units[unit]
-        far_product(kind, pair * PAIR, PAIR)
-        if kind != QUERY:
-            share_beacons(kind, pair)
-
-    def far_chunk(index):
-        kind, block = chunks[index]
-        far_product(kind, block * CHUNK, CHUNK)
-
-    work = {step: [] for step in range(count + 2)}
-    work[0] += [functools.partial(make_hidden, 2), functools.partial(make_hidden, 3)]
-    near_at = [1, 1, 2, 2, 4, 4]
-    for unit in range(len(units)):
-        work[near_at[min(unit, 5)]].append(functools.partial(near_product, unit))
-    for unit in range(len(units) - 1):
-        work[2 * unit + 3].append(functools.partial(far_unit, unit))
-    for pair in range(pairs - 1):
-        ready = 6 * pair + 8
-        work[ready - 1].append(functools.partial(await_beacons, pair))
-        work[ready].append(functools.partial(attend, 2 * pair))
-        work[ready + 2].append(functools.partial(attend, 2 * pair + 1))
-    work[count].append(functools.partial(far_chunk, count - 2))
-    work[count].append(functools.partial(await_beacons, pairs - 1))
-    work[count].append(functools.partial(attend, 2 * pairs - 2))
-    work[count + 1].append(functools.partial(far_chunk, count - 1))
-    work[count + 1].append(functools.partial(attend, 2 * pairs - 1))
-
-    make_hidden(0)
-    make_hidden(1)
-    for step in range(count + 2):
-        if step < count:
-            x_copy(step).wait_recv()
+    last = units - 1
+
+    @pl.loop(0, 4)
+    def _(block):
+        make_hidden(block)
+
+    def forward_y(index):
+        y_copy(index).wait_recv()
+        cy_copy(index).start()
+        cx_copy(index).wait_recv()
+
+    @pl.loop(0, count + 2)
+    def _(step):
+        @pl.when(step < count)
+        def _():
+            x_copy(step, wq_hbm).wait_recv()
             y_copy(step).start()
             cx_copy(step).start()
-            if step + AHEAD < count:
-                x_copy(step).wait_send()
-                x_copy(step + AHEAD).start()
-        if 1 <= step <= count:
-            y_copy(step - 1).wait_recv()
-            cy_copy(step - 1).start()
-            cx_copy(step - 1).wait_recv()
-        if step >= 2:
+
+        @pl.when(step + AHEAD < count)
+        def _():
+            x_copy(step, wq_hbm).wait_send()
+            x_start(step + AHEAD)
+
+        @pl.when((step >= 1) & (step < count))
+        def _():
+            forward_y(step - 1)
+
+        @pl.when(step == count + 1)
+        def _():
+            forward_y(step - 2)
+
+        @pl.when(step >= 2)
+        def _():
             cy_copy(step - 2).wait_recv()
-        for task in work[step]:
-            task()
+
+        @pl.when(step < units)
+        def _():
+            near_product(step)
+
+        unit = (step - 3) // 2
+
+        @pl.when((step >= 3) & ((unit < last - 1) | (step == 2 * last + 1)))
+        def _():
+            kind, pair = unit_of(unit)
+            tile = (step - 3) % 2
+            far_product(kind, columns(pair, PAIR), tile)
+
+            @pl.when(unit == last - 1)
+            def _():
+                far_product(kind, columns(pair, PAIR), 1)
+
+            @pl.when((kind != QUERY) & ((tile == 1) | (unit == last - 1)))
+            def _():
+                share_beacons(kind, pair)
+
+        @pl.when(step >= count)
+        def _():
+            kind, block = chunk_of(step - 2)
+
+            @pl.loop(0, 2)
+            def _(tile):
+                far_product(kind, columns(block, CHUNK), tile)
+
+        phase = (step - 8) % 6
+        final = step >= count
+        ready = (step >= 8) & ((phase == 0) | (phase == 2)) & (step < count - 1)
+
+        @pl.when((ready & (phase == 0)) | (step == count))
+        def _():
+            await_beacons(jnp.where(final, pairs - 1, (step - 8) // 6))
+
+        @pl.when(ready | final)
+        def _():
+            attend(
+                jnp.where(
+                    final, 2 * pairs - 2 + step - count, (step - 8) // 6 * 2 + phase // 2
+                )
+            )
 
     for index in range(count):
         if index + AHEAD >= count:
-            x_copy(index).wait_send()
+            x_copy(index, sources[chunk_of(index)[0]]).wait_send()
         y_copy(index).wait_send()
         cx_copy(index).wait_send()
         cy_copy(index).wait_send()
-    for unit in range(len(units)):
+    for unit in range(units):
         own_remote(unit).wait_send()
     for pair in range(pairs):
         for kind in (KEY, VALUE):
@@ -521,8 +578,8 @@
     vmem = pl.BlockSpec(memory_space=pltpu.VMEM)
     return pl.pallas_call(
         song_kernel,
-        out_shape=jax.ShapeDtypeStruct((rows, width), jnp.bfloat16),
-        in_specs=[anywhere, vmem, vmem, anywhere, anywhere, anywhere],
+        out_shape=pltpu.VMEM((rows, width), jnp.bfloat16),
+        in_specs=[anywhere] * 6,
         out_specs=vmem,
         scratch_shapes=[
             pltpu.VMEM((rows, depth), jnp.bfloat16),
@@ -531,6 +588,9 @@
             pltpu.VMEM((3, rows, width), jnp.bfloat16),
             pltpu.VMEM((rows, tempo_table.shape[0]), jnp.bfloat16),
             pltpu.VMEM((2, pairs, slots, PAIR), jnp.bfloat16),
+            pltpu.VMEM((1, rows), jnp.int32),
+            pltpu.VMEM(tempo_table.shape, jnp.bfloat16),
+            dma((2,)),
             dma((4,)),
             dma((units,)),
             dma((chunks,)),

time: 62.6 us -> 60.2 us (0.962)
  local copies, waits for them, and re-layouts: 2.26 us -> 0.97 us
  Pallas kernels: 60.1 us -> 59.1 us
    unnamed x1, local copies, waits for them, and re-layouts: 2.26 us -> 0.97 us
    pallas_call x1, Pallas kernels: 60.1 us -> 59.1 us  [on_device_fused(): pl.pallas_call(song_kernel, out_shape=pltpu.VMEM((rows, width), jnp.bfloa...]
where the time goes in v2:
time: 60.2 us; the launch traced here: 60.1 us
  Pallas kernels  59.1 us (98%)
  local copies, waits for them, and re-layouts  0.97 us (2%)
    pallas_call x1, Pallas kernels, on_device_fused(): pl.pallas_call(song_kernel, out_shape=pltpu.VMEM((rows, width), jnp.bfloa...  59.1 us

profile of v2, /device:TPU:0, one launch (start us, length us, event | category | flops | bytes accessed | tf_op | source)
XLA Modules:
  0.0 60.1 jit_solution(10414971131853372950)
XLA Ops:
  0.0 59.1 %shard_map.64 = bf16[1024,512]{1,0:T(8,128)(2,1)S(1)} custom-call(bf16[1024,4096]{1,0:T(8,128)(2,1)} %tokens_hbm.1, s32[1,1024]{1,0:T(1,128)} %bitcast.1, bf16[64,4096]{1,0:T(8,128)(2,1)} %table_hbm.1, bf16[1024,512]{1,0:T(8,128)(2,1)} %wq_hbm.1, bf16[1024,512]{1,0:T(8,128)(2,1)} %wk_hbm.1, bf16[1024,512]{1,0:T(8,128)(2,1)} %wv_hbm.1), custom_call_target="tpu_custom_call" | custom-call | flops 12884901888 | bytes 20971520 | tf_op jit(solution)/shard_map/pallas_call | solution.py:579
  59.1 1.0 %copy.8 = bf16[1024,512]{1,0:T(8,128)(2,1)} copy(bf16[1024,512]{1,0:T(8,128)(2,1)S(1)} %shard_map.64) | data formatting | bytes 2097152
